TPU v7x, 32 devices: a whole 2x2x4 slice. The times are simulated.
32 devices in a mesh: parts: 2 (over x), node: 2 (over core), rank: 8 (over z, y).
Axes of the slice: x: 2, y: 2, z: 4, core: 2. Of those that a mesh axis runs over, the one named last changes fastest.
Arguments:
- grad_out: bfloat16 [4096, 3584], P(('parts', 'node', 'rank')), parts along dimension 0, may hold values from -6 to 6
- expert_ids: int32 [4096, 2], P(('parts', 'node', 'rank')), parts along dimension 0, may hold values from 0 to 3, all different within a row; in each aligned block of 128 rows (0 to 127, 128 to 255, ...) at most 96 rows name the same one
- scores: float32 [4096, 2], P(('parts', 'node', 'rank')), parts along dimension 0, may hold values from 0.05 to 0.95
- gate_weight: bfloat16 [16, 3584, 256], P(('node', 'rank')), may hold values from -0.09375 to 0.09375
- up_weight: bfloat16 [16, 3584, 256], P(('node', 'rank')), may hold values from -0.09375 to 0.09375
- down_weight: bfloat16 [16, 256, 3584], P(('node', 'rank')), may hold values from -0.1875 to 0.1875
- saved_gate: bfloat16 [32, 1536, 256], P(('parts', 'node', 'rank')), parts along dimension 0, may hold values from -6 to 6
- saved_up: bfloat16 [32, 1536, 256], P(('parts', 'node', 'rank')), parts along dimension 0, may hold values from -1.5 to 1.5
Outputs:
- grad_in: bfloat16 [4096, 3584], P(('parts', 'node', 'rank')), parts along dimension 0
- grad_logit: float32 [4096, 2], P(('parts', 'node', 'rank')), parts along dimension 0
There are 2 independent parts, one for each index of `parts`. A program takes and returns all parts, laid end to end along the dimension named above; an argument that names none is the same for every part. Nothing has to cross between parts.
Inputs may be any that keep to these rules, and one draw needn't show every extreme that they name: `expert_ids`: within the 128 tokens of one device no expert is chosen more than 96 times, a bound that some block reaches; a token's 2 experts differ.
All inputs are finite; a program needn't handle non-finite values.
Results may differ from a plain program's by a relative error of at most 0.0065.
Values may be sent and summed in bfloat16 or wider, within the bound.
A program may use at most 128 MiB of HBM per device.

v0:
```python
import jax
import jax.numpy as jnp
from jax import lax
from jax.sharding import PartitionSpec as P

SPLIT = 4


route_scale = 2.5


def from_partner(block, axis, distance):
    count = lax.axis_size(axis)
    route = []
    for low in range(count):
        high = low | 1 << distance
        if high != low and high < count:
            route += [(low, high), (high, low)]
    return lax.ppermute(block, axis, route)


def take_half(stacked, chosen, axis_number):
    return lax.dynamic_index_in_dim(stacked, chosen, axis_number, keepdims=False)


def on_device(
    grad_out, expert_ids, scores, gate_weight, up_weight, down_weight, saved_gate, saved_up
):
    token_count, feature_width = grad_out.shape
    top_count = expert_ids.shape[1]
    source_count = lax.axis_size("node") * lax.axis_size("rank")
    expert_count = source_count // SPLIT
    hidden_width = gate_weight.shape[2]
    capacity = saved_gate.shape[1] // source_count
    quarter = capacity // SPLIT
    holder = lax.axis_index("rank") % SPLIT
    flat_ids = expert_ids.reshape(-1)
    onehot = (flat_ids[:, None] == jnp.arange(expert_count, dtype=jnp.int32)[None, :]).astype(
        jnp.int32
    )
    slot_index = jnp.sum((jnp.cumsum(onehot, axis=0) - onehot) * onehot, axis=1)
    slot_block = slot_index // quarter
    slot_within = slot_index % quarter
    repeated = jnp.repeat(grad_out, top_count, axis=0)
    empty_rows = jnp.zeros((expert_count * capacity, feature_width), jnp.bfloat16)
    location = (slot_block * expert_count + flat_ids) * quarter + slot_within
    buffered = (
        empty_rows.at[location]
        .set(repeated)
        .reshape(SPLIT, expert_count, 1, quarter, feature_width)
    )
    outgoing = jnp.broadcast_to(buffered, (SPLIT, expert_count, SPLIT, quarter, feature_width))
    outgoing = outgoing.reshape(SPLIT, source_count, quarter, feature_width)
    arrived = lax.all_to_all(outgoing, ("node", "rank"), split_axis=1, concat_axis=1, tiled=True)
    flat_rows = arrived.reshape(-1, feature_width)

    def arranged(saved):
        ordered = saved[0].reshape(source_count, SPLIT, quarter, hidden_width).transpose(1, 0, 2, 3)
        return ordered.reshape(-1, hidden_width).astype(jnp.float32)

    gate_pre = arranged(saved_gate)
    up_pre = arranged(saved_up)
    contract = (((1,), (1,)), ((), ()))
    d_hidden = lax.dot_general(
        flat_rows, down_weight[0], contract, preferred_element_type=jnp.float32
    )
    gate_sigmoid = jax.nn.sigmoid(gate_pre)
    gate_act = gate_pre * gate_sigmoid
    product_part = jnp.sum(d_hidden * gate_act * up_pre, axis=1).astype(jnp.bfloat16)
    d_gate = (d_hidden * up_pre * gate_sigmoid * (1.0 + gate_pre * (1.0 - gate_sigmoid))).astype(
        jnp.bfloat16
    )
    d_up = (d_hidden * gate_act).astype(jnp.bfloat16)
    partial_sum = lax.dot_general(
        d_gate, gate_weight[0], contract, preferred_element_type=jnp.float32
    )
    partial_sum = partial_sum + lax.dot_general(
        d_up, up_weight[0], contract, preferred_element_type=jnp.float32
    )
    partial_rows = partial_sum.astype(jnp.bfloat16).reshape(
        2, 2, source_count, quarter, feature_width
    )
    partial_products = product_part.reshape(2, 2, source_count, quarter)
    low_bit = holder % 2
    high_bit = holder // 2
    kept_rows = take_half(partial_rows, low_bit, 1)
    sent_rows = take_half(partial_rows, 1 - low_bit, 1)
    kept_products = take_half(partial_products, low_bit, 1)
    sent_products = take_half(partial_products, 1 - low_bit, 1)
    came_rows, came_products = from_partner((sent_rows, sent_products), "rank", 0)
    pair_rows = kept_rows.astype(jnp.float32) + came_rows.astype(jnp.float32)
    pair_products = kept_products.astype(jnp.float32) + came_products.astype(jnp.float32)
    kept_pair = take_half(pair_rows, high_bit, 0)
    sent_pair = take_half(pair_rows, 1 - high_bit, 0)
    kept_pair_products = take_half(pair_products, high_bit, 0)
    sent_pair_products = take_half(pair_products, 1 - high_bit, 0)
    came_pair, came_pair_products = from_partner((sent_pair, sent_pair_products), "rank", 1)
    summed_rows = (kept_pair + came_pair).astype(jnp.bfloat16)
    summed_products = (kept_pair_products + came_pair_products).astype(jnp.bfloat16)
    returned_rows, returned_products = (
        lax.all_to_all(summed_rows, ("node", "rank"), split_axis=0, concat_axis=0, tiled=True),
        lax.all_to_all(summed_products, ("node", "rank"), split_axis=0, concat_axis=0, tiled=True),
    )
    returned_rows = returned_rows.reshape(expert_count * capacity, feature_width)
    returned_products = returned_products.reshape(-1)
    gathered_at = flat_ids * capacity + slot_index
    picked = (
        returned_rows[gathered_at]
        .reshape(token_count, top_count, feature_width)
        .astype(jnp.float32)
    )
    picked_products = (
        returned_products[gathered_at].reshape(token_count, top_count).astype(jnp.float32)
    )
    score_total = jnp.sum(scores, axis=1, keepdims=True)
    weights = route_scale * scores / score_total
    grad_in = jnp.sum(weights[:, :, None] * picked, axis=1).astype(jnp.bfloat16)
    centred = (
        picked_products - jnp.sum(picked_products * scores, axis=1, keepdims=True) / score_total
    )
    grad_logit = route_scale / score_total * centred * scores * (1.0 - scores)
    return (grad_in, grad_logit)


def solution(mesh):
    in_specs = (
        P(("parts", "node", "rank"), None),
        P(("parts", "node", "rank"), None),
        P(("parts", "node", "rank"), None),
        P(("node", "rank"), None, None),
        P(("node", "rank"), None, None),
        P(("node", "rank"), None, None),
        P(("parts", "node", "rank"), None, None),
        P(("parts", "node", "rank"), None, None),
    )
    out_specs = (P(("parts", "node", "rank"), None), P(("parts", "node", "rank"), None))
    return jax.shard_map(
        on_device, mesh=mesh, in_specs=in_specs, out_specs=out_specs, check_vma=False
    )
```

profile of v0, /device:TPU:0, one launch (start us, length us, event | category | flops | bytes accessed | tf_op | source)
XLA Modules:
  0.0 668.5 jit_solution(9875730412388857350)
XLA Ops:
  0.6 0.0 copy-start
  0.6 0.9 copy.93
  1.6 0.1 eq.34
  1.7 0.1 eq.30
  1.8 0.1 reshape.177
  2.0 1.2 reduce-window.6
  3.2 0.1 slice.12
  3.3 0.1 copy.95
  3.4 0.1 copy.96
  3.5 0.1 add_bitcast_fusion
  3.6 3.4 broadcast_in_dim.9
  7.0 4.9 reshape.212
  12.0 6.0 scatter_custom_fusion
  17.9 3.6 copy.98
  21.6 7.1 %broadcast_in_dim.11 = bf16[4,4,4,24,3584]{4,3,0,2,1:T(8,128)(2,1)} broadcast(bf16[4,4,24,3584]{3,2,0,1:T(8,128)(2,1)} %copy.98), dimensions={0,1,3,4} | broadcast | bytes 13762560 | tf_op jit(solution)/shard_map/broadcast_in_dim | solution.py:52
  28.6 7.6 %all-to-all-start = ((bf16[4,16,24,3584]{3,2,0,1:T(8,128)(2,1)}), bf16[4,16,24,3584]{3,2,0,1:T(8,128)(2,1)}, u32[]{:S(2)}, u32[]{:S(2)}) async-start(bf16[4,16,24,3584]{3,2,0,1:T(8,128)(2,1)} %bitcast.77), calls=%async_computation | async-start | bytes 22020096 | tf_op jit(solution)/shard_map/all_to_all | solution.py:54
  36.2 0.0 copy-done.5
  36.2 0.2 convert_bitcast_fusion
  36.4 1.4 copy.102
  37.8 1.9 copy.103
  39.7 1.3 convert_bitcast_fusion.1
  41.0 1.3 copy.100
  42.3 3.1 copy.101
  45.3 217.6 %all-to-all-done = bf16[4,16,24,3584]{3,2,0,1:T(8,128)(2,1)} async-done(((bf16[4,16,24,3584]{3,2,0,1:T(8,128)(2,1)}), bf16[4,16,24,3584]{3,2,0,1:T(8,128)(2,1)}, u32[]{:S(2)}, u32[]{:S(2)}) %all-to-all-start) | async-done | bytes 11010080 | tf_op jit(solution)/shard_map/all_to_all | solution.py:54
  262.9 6.2 copy.99
  269.1 0.0 copy-done.4
  269.1 0.0 copy-done.7
  269.1 3.2 multiply_reduce_fusion.1
  272.4 0.0 copy-start.3
  272.4 1.1 copy-done.3
  273.5 0.0 copy-done
  273.5 9.6 %fusion.2 = f32[1536,3584]{1,0:T(8,128)} fusion(bf16[1,3584,256]{2,1,0:T(8,128)(2,1)S(1)} %copy-done, f32[1536,256]{0,1:T(8,128)S(1)} %copy.103, f32[1536,256]{0,1:T(8,128)S(1)} %get-tuple-element.17, f32[1536,256]{0,1:T(8,128)S(1)} %copy-done.4), kind=kOutput, calls=%fused_computation.11 | convolution fusion | flops 2822504448 | bytes 28573696 | tf_op jit(solution)/shard_map/dot_general | solution.py:74
  283.1 15.6 %add_convert_fusion = bf16[1536,3584]{1,0:T(8,128)(2,1)} fusion(f32[1536,3584]{1,0:T(8,128)} %fusion.2, bf16[1,3584,256]{2,1,0:T(8,128)(2,1)} %param.12, f32[1536,256]{0,1:T(8,128)} %copy-done.3, f32[1536,256]{0,1:T(8,128)S(1)} %copy.103), kind=kOutput, calls=%fused_computation.3 | convolution fusion | flops 2831941632 | bytes 38010880 | tf_op jit(solution)/shard_map/dot_general | solution.py:77
  298.7 5.4 dynamic-slice_bitcast_fusion.1
  304.1 0.6 collective-permute-start
  304.7 119.5 %collective-permute-done = bf16[2,16,24,3584]{3,2,1,0:T(8,128)(2,1)} collective-permute-done((bf16[2,16,24,3584]{3,2,1,0:T(8,128)(2,1)}, bf16[2,16,24,3584]{3,2,1,0:T(8,128)(2,1)}, u32[]{:S(2)}, u32[]{:S(2)}) %collective-permute-start) | collective-permute-done | bytes 5505056 | tf_op jit(solution)/shard_map/ppermute | solution.py:19
  424.1 5.8 convert_add_fusion
  430.0 0.0 copy-start.2
  430.0 3.0 dynamic-slice_bitcast_fusion
  433.0 2.9 copy-done.2
  435.9 15.3 %collective-permute-start.1 = (f32[16,24,3584]{2,1,0:T(8,128)}, f32[16,24,3584]{2,1,0:T(8,128)}, u32[]{:S(2)}, u32[]{:S(2)}) collective-permute-start(f32[16,24,3584]{2,1,0:T(8,128)} %dynamic-slice_bitcast_fusion), channel_id=1, source_target_pairs={{0,2},{2,0},{1,3},{3,1},{4,6},{6,4},{5,7},{7,5},{8,10},{10,8},{9,1... | collective-permute-start | bytes 16515080 | tf_op jit(solution)/shard_map/ppermute | solution.py:19
  451.2 0.1 convert_element_type.107
  451.4 0.6 collective-permute-start.2
  452.0 3.1 collective-permute-done.2
  455.1 0.0 collective-permute-start.3
  455.1 114.1 %collective-permute-done.3 = f32[16,24]{1,0:T(8,128)S(1)} collective-permute-done((f32[16,24]{1,0:T(8,128)S(1)}, f32[16,24]{1,0:T(8,128)S(1)}, u32[]{:S(2)}, u32[]{:S(2)}) %collective-permute-start.3) | collective-permute-done | bytes 1568 | tf_op jit(solution)/shard_map/ppermute | solution.py:19
  569.2 0.6 copy.107
  569.8 4.8 all-to-all-start.2
  574.6 0.0 collective-permute-done.1
  574.6 6.4 fusion
  581.0 0.0 all-to-all-done.2
  581.0 6.2 all-to-all-start.1
  587.2 0.1 copy.108
  587.4 0.1 reshape.183
  587.5 1.9 gather_fusion.1
  589.4 0.1 reshape.189
  589.5 0.1 copy.109
  589.6 0.1 multiply_reduce_fusion.2
  589.7 0.6 subtract_multiply_fusion
  590.3 0.1 copy.92
  590.4 57.6 %all-to-all-done.1 = bf16[16,24,3584]{2,1,0:T(8,128)(2,1)} async-done(((bf16[16,24,3584]{2,1,0:T(8,128)(2,1)}), bf16[16,24,3584]{2,1,0:T(8,128)(2,1)}, u32[]{:S(2)}, u32[]{:S(2)}) %all-to-all-start.1) | async-done | bytes 2752544 | tf_op jit(solution)/shard_map/all_to_all | solution.py:101
  648.0 6.9 %gather_fusion = bf16[256,3584]{1,0:T(8,128)(2,1)} fusion(bf16[384,3584]{1,0:T(8,128)(2,1)} %bitcast.21, s32[1024]{0:T(1024)S(1)} %pad_clamp_fusion), kind=kCustom, calls=%fused_computation | custom fusion | bytes 3671040 | tf_op jit(solution)/shard_map/gather | solution.py:108
  654.9 5.3 reshape.187
  660.3 8.2 %multiply_reduce_fusion = bf16[128,3584]{1,0:T(8,128)(2,1)} fusion(f32[128,2,3584]{2,1,0:T(2,128)} %reshape.187, f32[128,2]{1,0:T(8,128)S(1)} %copy.92), kind=kLoop, calls=%fused_computation.9 | loop fusion | flops 1376256 | bytes 4588544 | tf_op jit(solution)/shard_map/reduce_sum | solution.py:117
  (20 shorter events, 0.2 us)
Async XLA Ops:
  0.6 272.9 %copy-start = (bf16[1,3584,256]{2,1,0:T(8,128)(2,1)S(1)}, bf16[1,3584,256]{2,1,0:T(8,128)(2,1)}, u32[]{:S(2)}) copy-start(bf16[1,3584,256]{2,1,0:T(8,128)(2,1)} %param.11) | copy-start | bytes 5505028
  28.6 7.6 %copy-start.5 = (bf16[1,1536,256]{2,1,0:T(8,128)(2,1)S(1)}, bf16[1,1536,256]{2,1,0:T(8,128)(2,1)}, u32[]{:S(2)}) copy-start(bf16[1,1536,256]{2,1,0:T(8,128)(2,1)} %param.14) | copy-start | bytes 2359300
  28.6 234.3 %all-to-all-start = ((bf16[4,16,24,3584]{3,2,0,1:T(8,128)(2,1)}), bf16[4,16,24,3584]{3,2,0,1:T(8,128)(2,1)}, u32[]{:S(2)}, u32[]{:S(2)}) async-start(bf16[4,16,24,3584]{3,2,0,1:T(8,128)(2,1)} %bitcast.77), calls=%async_computation | async-start | bytes 22020096 | tf_op jit(solution)/shard_map/all_to_all | solution.py:54
  262.9 6.2 copy-start.4
  262.9 6.2 copy-start.7
  272.4 1.2 copy-start.3
  304.1 120.0 %collective-permute-start = (bf16[2,16,24,3584]{3,2,1,0:T(8,128)(2,1)}, bf16[2,16,24,3584]{3,2,1,0:T(8,128)(2,1)}, u32[]{:S(2)}, u32[]{:S(2)}) collective-permute-start(bf16[2,16,24,3584]{3,2,1,0:T(8,128)(2,1)} %dynamic-slice_bitcast_fusion.1), channel_id=1, source_target_pairs={{0,1},{1,0},{2,3},{3,2},{4,5},{5,4},{6,7},{7,6},{8,9},{9,8},{10,11... | collective-permute-start | bytes 16515080 | tf_op jit(solution)/shard_map/ppermute | solution.py:19
  430.0 5.9 copy-start.2
  435.9 138.7 %collective-permute-start.1 = (f32[16,24,3584]{2,1,0:T(8,128)}, f32[16,24,3584]{2,1,0:T(8,128)}, u32[]{:S(2)}, u32[]{:S(2)}) collective-permute-start(f32[16,24,3584]{2,1,0:T(8,128)} %dynamic-slice_bitcast_fusion), channel_id=1, source_target_pairs={{0,2},{2,0},{1,3},{3,1},{4,6},{6,4},{5,7},{7,5},{8,10},{10,8},{9,1... | collective-permute-start | bytes 16515080 | tf_op jit(solution)/shard_map/ppermute | solution.py:19
  451.4 3.7 collective-permute-start.2
  455.1 114.1 %collective-permute-start.3 = (f32[16,24]{1,0:T(8,128)S(1)}, f32[16,24]{1,0:T(8,128)S(1)}, u32[]{:S(2)}, u32[]{:S(2)}) collective-permute-start(f32[16,24]{1,0:T(8,128)S(1)} %dynamic-slice_bitcast_fusion.2), channel_id=1, source_target_pairs={{0,2},{2,0},{1,3},{3,1},{4,6},{6,4},{5,7},{7,5},{8,10},{10,8},{9,1... | collective-permute-start | bytes 4616 | tf_op jit(solution)/shard_map/ppermute | solution.py:19
  569.8 11.2 %all-to-all-start.2 = ((bf16[16,1,24]{2,1,0:T(2,128)(2,1)}), bf16[16,1,24]{2,1,0:T(2,128)(2,1)S(1)}, u32[]{:S(2)}, u32[]{:S(2)}) async-start(bf16[16,1,24]{2,1,0:T(2,128)(2,1)} %copy.107), calls=%async_computation.2 | async-start | bytes 16384 | tf_op jit(solution)/shard_map/all_to_all | solution.py:102
  581.0 6.2 copy-start.6
  581.0 67.0 %all-to-all-start.1 = ((bf16[16,24,3584]{2,1,0:T(8,128)(2,1)}), bf16[16,24,3584]{2,1,0:T(8,128)(2,1)}, u32[]{:S(2)}, u32[]{:S(2)}) async-start(bf16[16,24,3584]{2,1,0:T(8,128)(2,1)} %fusion), calls=%async_computation.1 | async-start | bytes 5505024 | tf_op jit(solution)/shard_map/all_to_all | solution.py:101
  654.9 13.5 %copy-start.1 = (bf16[1,3584,256]{2,1,0:T(8,128)(2,1)S(1)}, bf16[1,3584,256]{2,1,0:T(8,128)(2,1)}, u32[]{:S(2)}) copy-start(bf16[1,3584,256]{2,1,0:T(8,128)(2,1)} %param.11) | copy-start | bytes 5505028
where the time goes:
time: 670 us; the launch traced here: 668 us
  waiting for transfers between devices  512 us (76%)
  local copies, waits for them, and re-layouts  68.3 us (10%)
  starting transfers between devices  35 us (5%)
  matrix products  28.4 us (4%)
  other arithmetic  24.1 us (4%)
    ppermute x4, waiting for transfers between devices, from_partner(): return lax.ppermute(block, axis, route)  237 us
    all_to_all x1, waiting for transfers between devices, on_device(): lax.all_to_all(outgoing, ('node', 'rank'), split_axis=1, concat_axis=1, t...  218 us
    all_to_all x1, waiting for transfers between devices, on_device(): lax.all_to_all(summed_rows, ('node', 'rank'), split_axis=0, concat_axis=0...  57.6 us
    ppermute x4, starting transfers between devices, from_partner(): return lax.ppermute(block, axis, route)  16.5 us
    dot_general x1, matrix products, on_device(): lax.dot_general(d_up, up_weight[0], contract, preferred_element_type=jnp....  15.6 us
  transfers between devices with their start and end apart: 7, of which 5 were waited for; matrix products, arithmetic and copies ran while one was open for 3% of the time, Pallas kernels for 0%

commit v1 on v0

--- a/solution.py
+++ b/solution.py
@@ -122,6 +122,59 @@
     return (grad_in, grad_logit)
 
 
+def token_order(ids, scores, expert, capacity):
+    lead = ids.shape[0]
+    mine = jnp.any(ids == expert, axis=-1)
+    slots = jnp.cumsum(mine.astype(jnp.int32), axis=1) - 1
+    slots = jnp.where(mine, slots, -1)
+    total = jnp.sum(scores, axis=-1)
+    weight = jnp.sum(jnp.where(ids == expert, scores, 0.0), axis=-1) * route_scale / total
+    pick = (slots[:, :, None] == jnp.arange(capacity)[None, None, :]).astype(jnp.bfloat16)
+    return pick, weight
+
+
+def dense_on_device(
+    grad_out, expert_ids, scores, gate_weight, up_weight, down_weight, saved_gate, saved_up
+):
+    axes = ("node", "rank")
+    token_count, feature_width = grad_out.shape
+    source_count = lax.axis_size("node") * lax.axis_size("rank")
+    expert_count = source_count // SPLIT
+    hidden = gate_weight.shape[2]
+    capacity = saved_gate.shape[1] // source_count
+    expert = lax.axis_index(axes) // SPLIT
+    rows = lax.all_gather(grad_out, axes, axis=0, tiled=True)
+    ids = lax.all_gather(expert_ids, axes, axis=0, tiled=False)
+    all_scores = lax.all_gather(scores, axes, axis=0, tiled=False)
+    pick, weight = token_order(ids, all_scores, expert, capacity)
+
+    def spread(saved):
+        by_source = saved[0].reshape(source_count, capacity, hidden)
+        return jnp.einsum("stc,sch->sth", pick, by_source, preferred_element_type=jnp.float32).reshape(-1, hidden)
+
+    g = spread(saved_gate)
+    u = spread(saved_up)
+    contract = (((1,), (1,)), ((), ()))
+    d_hidden = lax.dot_general(rows, down_weight[0], contract, preferred_element_type=jnp.float32)
+    sig = jax.nn.sigmoid(g)
+    act = g * sig
+    part = jnp.sum(d_hidden * act * u, axis=1)
+    scaled = d_hidden * weight.reshape(-1, 1)
+    d_gate = (scaled * u * sig * (1.0 + g * (1.0 - sig))).astype(jnp.bfloat16)
+    d_up = (scaled * act).astype(jnp.bfloat16)
+    both = jnp.concatenate([d_gate, d_up], axis=1)
+    weights = jnp.concatenate([gate_weight[0], up_weight[0]], axis=1)
+    partial = lax.dot_general(both, weights, contract, preferred_element_type=jnp.float32)
+    grad_in = lax.psum_scatter(partial.astype(jnp.bfloat16), axes, scatter_dimension=0, tiled=True)
+    lanes = jnp.where(jnp.arange(expert_count)[None, :] == expert, part[:, None], 0.0)
+    products = lax.psum_scatter(lanes, axes, scatter_dimension=0, tiled=True)
+    picked = jnp.sum(jnp.where(expert_ids[:, :, None] == jnp.arange(expert_count)[None, None, :], products[:, None, :], 0.0), axis=2)
+    total = jnp.sum(scores, axis=1, keepdims=True)
+    centred = picked - jnp.sum(picked * scores, axis=1, keepdims=True) / total
+    grad_logit = route_scale / total * centred * scores * (1.0 - scores)
+    return grad_in, grad_logit
+
+
 def solution(mesh):
     in_specs = (
         P(("parts", "node", "rank"), None),
@@ -134,6 +187,7 @@
         P(("parts", "node", "rank"), None, None),
     )
     out_specs = (P(("parts", "node", "rank"), None), P(("parts", "node", "rank"), None))
+    few = mesh.shape["node"] * mesh.shape["rank"] <= 16
     return jax.shard_map(
-        on_device, mesh=mesh, in_specs=in_specs, out_specs=out_specs, check_vma=False
+        dense_on_device if few else on_device, mesh=mesh, in_specs=in_specs, out_specs=out_specs, check_vma=False
     )

time: 670 us -> 362 us (0.54)
  waiting for transfers between devices: 512 us -> 240 us
  blocking collectives: 0 us -> 63.8 us
  local copies, waits for them, and re-layouts: 68.3 us -> 8.22 us
  starting transfers between devices: 35 us -> 0.12 us
  other arithmetic: 24.1 us -> 1.1 us
  between operations: 0.89 us -> 13.8 us
    all_to_all x3 -> x0, waiting for transfers between devices: 275 us -> none  [the longest x1 218 us: on_device(): lax.all_to_all(outgoing, ('node', 'rank'), split_axis=1, concat_axis=1, t...]
    ppermute x4 -> x0, waiting for transfers between devices: 237 us -> none  [from_partner(): return lax.ppermute(block, axis, route)]
    reduce_scatter x0 -> x1, waiting for transfers between devices: none -> 152 us  [dense_on_device(): lax.psum_scatter(partial.astype(jnp.bfloat16), axes, scatter_dimension=0,...]
    all_gather x0 -> x2, blocking collectives: none -> 63.8 us  [the longest x1 34.9 us: dense_on_device(): ids = lax.all_gather(expert_ids, axes, axis=0, tiled=False)]
    all_gather x0 -> x1, waiting for transfers between devices: none -> 44.2 us  [dense_on_device(): rows = lax.all_gather(grad_out, axes, axis=0, tiled=True)]
    unnamed x0 -> x4, waiting for transfers between devices: none -> 43.5 us
    all_to_all x3 -> x0, starting transfers between devices: 18.5 us -> none  [the longest x1 7.57 us: on_device(): lax.all_to_all(outgoing, ('node', 'rank'), split_axis=1, concat_axis=1, t...]
    ppermute x4 -> x0, starting transfers between devices: 16.5 us -> none  [from_partner(): return lax.ppermute(block, axis, route)]
  transfers between devices with their start and end apart: 7 -> 3, of which waited for: 5 -> 3; matrix products, arithmetic and copies ran while one was open for 3% -> 7% of each run, Pallas kernels for 0% -> 0%
where the time goes in v1:
time: 362 us; the launch traced here: 361 us
  waiting for transfers between devices  240 us (66%)
  blocking collectives  63.8 us (18%)
  matrix products  34.2 us (9%)
  between operations  13.8 us (4%)
  local copies, waits for them, and re-layouts  8.22 us (2%)
    reduce_scatter x1, waiting for transfers between devices, dense_on_device(): lax.psum_scatter(partial.astype(jnp.bfloat16), axes, scatter_dimension=0,...  152 us
    all_gather x1, waiting for transfers between devices, dense_on_device(): rows = lax.all_gather(grad_out, axes, axis=0, tiled=True)  44.2 us
    unnamed x4, waiting for transfers between devices  43.5 us
    all_gather x1, blocking collectives, dense_on_device(): ids = lax.all_gather(expert_ids, axes, axis=0, tiled=False)  34.9 us
    all_gather x1, blocking collectives, dense_on_device(): all_scores = lax.all_gather(scores, axes, axis=0, tiled=False)  29 us
    dot_general x1, matrix products, dense_on_device(): lax.dot_general(rows, down_weight[0], contract, preferred_element_type=jn...  16.5 us
    dot_general x1, matrix products, dense_on_device(): lax.dot_general(both, weights, contract, preferred_element_type=jnp.float32)  12.9 us
  transfers between devices with their start and end apart: 3, of which 3 were waited for; matrix products, arithmetic and copies ran while one was open for 7% of the time, Pallas kernels for 0%

profile of v1, /device:TPU:0, one launch (start us, length us, event | category | flops | bytes accessed | tf_op | source)
XLA Modules:
  0.0 361.2 jit_solution(11349079516335703780)
XLA Ops:
  7.2 0.0 copy-start
  7.2 0.0 all-gather.4.cloned.1.call-start
  7.2 0.7 all-gather.4.cloned.1.call-update
  7.9 0.0 reduce-scatter.7.cloned.1.call-start
  8.0 34.9 %all-gather = s32[2048,2]{0,1:T(2,128)S(1)} all-gather(s32[128,2]{0,1:T(2,128)} %param.9), channel_id=2, replica_groups=mesh['parts'=2,'node'=2,'rank'=8] {'node','rank'}, dimensions={0}, use_global_device_ids=true | all-gather | bytes 17408 | tf_op jit(solution)/shard_map/all_gather | solution.py:147
  42.9 0.3 reduce_window_sum.11
  43.2 3.0 fusion.9
  46.2 0.0 copy-start.1
  46.2 3.0 copy.18
  49.2 0.0 copy-done.1
  49.2 1.8 fusion.10
  50.9 0.0 copy-start.2
  50.9 3.0 copy.17
  53.9 0.0 copy-done.2
  53.9 29.0 %all-gather.1 = f32[2048,2]{0,1:T(2,128)S(1)} all-gather(f32[128,2]{0,1:T(2,128)S(1)} %copy-done.2), channel_id=3, replica_groups=mesh['parts'=2,'node'=2,'rank'=8] {'node','rank'}, dimensions={0}, use_global_device_ids=true | all-gather | bytes 17408 | tf_op jit(solution)/shard_map/all_gather | solution.py:148
  82.9 44.2 %all-gather.4.cloned.1.call-done = bf16[2048,3584]{1,0:T(8,128)(2,1)} async-done(((bf16[128,3584]{1,0:T(8,128)(2,1)}), bf16[2048,3584]{1,0:T(8,128)(2,1)}) %all-gather.4.cloned.1.call-update) | async-done | bytes 14680080 | tf_op jit(solution)/shard_map/all_gather | solution.py:146
  127.2 0.0 copy-done
  127.2 16.5 %multiply_reduce_fusion = (f32[2048]{0:T(1024)S(1)}, bf16[2048,256]{0,1:T(8,128)(2,1)S(1)}, bf16[2048,256]{0,1:T(8,128)(2,1)}) fusion(f32[2048,256]{0,1:T(8,128)} %copy.17, f32[2048,256]{0,1:T(8,128)} %copy.18, f32[2048]{0:T(1024)S(1)} %multiply_divide_fusion, bf16[2048,3584]{1,0:T(8,128)(2,1)} %all-gather.4.cloned.1.call-done, ...), kind=kOutput, calls=%fused_computation.7 | convolution fusion | flops 3767007232 | bytes 22822912 | tf_op jit(solution)/shard_map/dot_general | solution.py:158
  143.7 0.1 broadcast_select_fusion
  143.7 1.4 copy.19
  145.1 0.0 reduce-scatter.7.cloned.1.call-update
  145.1 0.0 reduce-scatter.5.cloned.1.call-start
  145.2 12.9 %convolution_convert_fusion = bf16[2048,3584]{1,0:T(8,128)(2,1)} fusion(bf16[3584,256]{1,0:T(8,128)(2,1)} %bitcast.22, bf16[3584,256]{1,0:T(8,128)(2,1)} %bitcast.23, bf16[2048,256]{0,1:T(8,128)(2,1)} %get-tuple-element.8, bf16[2048,256]{0,1:T(8,128)(2,1)S(1)} %get-tuple-element.7), kind=kOutput, calls=%fused_computation | convolution fusion | flops 7535067136 | bytes 20447232 | tf_op jit(solution)/shard_map/dot_general | solution.py:167
  158.1 0.0 copy-start.3
  158.1 0.0 reduce-scatter.5.cloned.1.call-update
  158.1 42.8 %reduce-scatter.7.cloned.1.call-done = f32[128,4]{1,0:T(8,128)} async-done(((f32[2048,4]{1,0:T(8,128)}), f32[128,4]{1,0:T(8,128)}) %reduce-scatter.7.cloned.1.call-update) | async-done | bytes 2064
  200.9 0.9 copy.20
  201.8 0.0 copy-done.3
  201.9 0.6 subtract_multiply_fusion
  202.4 152.2 %reduce-scatter.5.cloned.1.call-done = bf16[128,3584]{1,0:T(8,128)(2,1)} async-done(((bf16[2048,3584]{1,0:T(8,128)(2,1)}), bf16[128,3584]{1,0:T(8,128)(2,1)}) %reduce-scatter.5.cloned.1.call-update) | async-done | bytes 917520 | tf_op jit(solution)/shard_map/reduce_scatter | solution.py:168
  (9 shorter events, 0.2 us)
Async XLA Ops:
  7.2 120.0 %copy-start = (bf16[1,256,3584]{2,1,0:T(8,128)(2,1)S(1)}, bf16[1,256,3584]{2,1,0:T(8,128)(2,1)}, u32[]{:S(2)}) copy-start(bf16[1,256,3584]{2,1,0:T(8,128)(2,1)} %param.13) | copy-start | bytes 5505028
  7.2 120.0 %all-gather.4.cloned.1.call-start = ((), (), s32[]{:S(2)}) async-start(), calls=%async_computation.2 | async-start | bytes 15597568 | tf_op jit(solution)/shard_map/all_gather | solution.py:146
  7.9 193.0 %reduce-scatter.7.cloned.1.call-start = ((), (), s32[]{:S(2)}) async-start(), calls=%async_computation.4 | async-start | bytes 1114112
  46.2 3.0 copy-start.1
  50.9 3.0 copy-start.2
  145.1 209.6 %reduce-scatter.5.cloned.1.call-start = ((), (), s32[]{:S(2)}) async-start(), calls=%async_computation.3 | async-start | bytes 15597568 | tf_op jit(solution)/shard_map/reduce_scatter | solution.py:168
  158.1 43.7 %copy-start.3 = (s32[128,2]{0,1:T(2,128)S(1)}, s32[128,2]{0,1:T(2,128)}, u32[]{:S(2)}) copy-start(s32[128,2]{0,1:T(2,128)} %param.9) | copy-start | bytes 3076
Sparse Core Ops, SparseCore 0:
  10.2 116.8 all-gather.3
  145.2 55.6 reduce-scatter.6
  206.1 148.5 reduce-scatter.4

commit v2 on v0

--- a/solution.py
+++ b/solution.py
@@ -1,6 +1,8 @@
 import jax
 import jax.numpy as jnp
 from jax import lax
+from jax.experimental import pallas as pl
+from jax.experimental.pallas import tpu as pltpu
 from jax.sharding import PartitionSpec as P
 
 SPLIT = 4
@@ -122,6 +124,472 @@
     return (grad_in, grad_logit)
 
 
+MESH = pl.DeviceIdType.MESH
+F32 = jnp.float32
+BF16 = jnp.bfloat16
+NT = (((1,), (1,)), ((), ()))
+NN = (((1,), (0,)), ((), ()))
+WIDE = 512
+ZS = 4
+
+
+def dot(a, b, how):
+    return lax.dot_general(a, b, how, preferred_element_type=F32)
+
+
+def fused(
+    ids_ref, scores_ref, x_hbm, gate_hbm, up_hbm, down_hbm, sg_hbm, su_hbm,
+    out_ref, prod_ref,
+    X, WD, WG, WU, SG, SU, META, DGU, QF, SS, SR, UPIN, DNIN, UPOUT, DNOUT, FIN, PRS, PRR,
+    loc_sem, y_send, y_recv, x_send, x_recv, ag_send, ag_recv, sib_send, sib_recv,
+    meta_send, meta_recv, pr_send, pr_recv, cs_send, cs_recv, u_send, u_recv, d_send, d_recv,
+):
+    T, D = x_hbm.shape
+    H = gate_hbm.shape[1]
+    CAP = SG.shape[3]
+    NK = D // WIDE
+    x = lax.axis_index("parts")
+    c = lax.axis_index("node")
+    r = lax.axis_index("rank")
+    z = r // 2
+    y = r % 2
+    me = z * 2 + c
+    expert = c * 2 + z // 2
+
+    sibling = (x, 1 - c, r)
+    y_peer = (x, c, z * 2 + 1 - y)
+    x_peer = (1 - x, c, r)
+    above = (x, c, jnp.minimum(z + 1, ZS - 1) * 2 + y)
+    below = (x, c, jnp.maximum(z - 1, 0) * 2 + y)
+
+    def column(o):
+        p = (me + o) % 8
+        return (x, p % 2, (p // 2) * 2 + y)
+
+    def remote(src, dst, send, recv, peer):
+        return pltpu.make_async_remote_copy(
+            src_ref=src, dst_ref=dst, send_sem=send, recv_sem=recv, device_id=peer, device_id_type=MESH
+        )
+
+    barrier = pltpu.get_barrier_semaphore()
+    for peer in [y_peer, x_peer] + [column(o) for o in range(1, 8)]:
+        pl.semaphore_signal(barrier, inc=1, device_id=peer, device_id_type=MESH)
+    pl.semaphore_wait(barrier, 9)
+
+    def chunk(zz):
+        return X.at[zz, pl.ds(pl.multiple_of(c * T, T), T)]
+
+    def chunk_other(zz):
+        return X.at[zz, pl.ds(pl.multiple_of((1 - c) * T, T), T)]
+
+    def up_copy(d, src):
+        return remote(src, chunk(z - d), ag_send.at[0, d], ag_recv.at[0, d], above)
+
+    def down_copy(d, src):
+        return remote(src, chunk(z + d), ag_send.at[1, d], ag_recv.at[1, d], below)
+
+    def up_arrival(d):
+        return remote(chunk(z - d), chunk(z - d), ag_send.at[0, d - 1], ag_recv.at[0, d - 1], below)
+
+    def down_arrival(d):
+        return remote(chunk(z + d), chunk(z + d), ag_send.at[1, d - 1], ag_recv.at[1, d - 1], above)
+
+    def sib_copy(n, zz, src):
+        return remote(src, chunk(zz), sib_send.at[n], sib_recv.at[n], sibling)
+
+    def sib_arrival(n, zz):
+        return remote(chunk_other(zz), chunk_other(zz), sib_send.at[n], sib_recv.at[n], sibling)
+
+    @pl.when(z < ZS - 1)
+    def _():
+        up_copy(0, x_hbm).start()
+
+    @pl.when(z > 0)
+    def _():
+        down_copy(0, x_hbm).start()
+
+    def piece(n):
+        if n == 0:
+            half = pl.ds(pl.multiple_of(x * (H // 2), H // 2), H // 2)
+            return down_hbm.at[half], WD.at[1, half]
+        if n == 1:
+            return sg_hbm.at[:, :, 1 - y], SG.at[1]
+        return su_hbm.at[:, :, 1 - y], SU.at[1]
+
+    def y_copy(n):
+        src, dst = piece(n)
+        return remote(src, dst, y_send.at[n], y_recv.at[n], y_peer)
+
+    def y_arrival(n):
+        dst = piece(n)[1]
+        return remote(dst, dst, y_send.at[n], y_recv.at[n], y_peer)
+
+    def rows_of(k, which):
+        return pl.ds(pl.multiple_of(k * WIDE + which * (WIDE // 2), WIDE // 2), WIDE // 2)
+
+    def gu_copies(k):
+        rows = rows_of(k, x)
+        return [
+            remote(gate_hbm.at[rows], WG.at[1, rows], y_send.at[3 + k], y_recv.at[3 + k], y_peer),
+            remote(up_hbm.at[rows], WU.at[1, rows], y_send.at[3 + NK + k], y_recv.at[3 + NK + k], y_peer),
+        ]
+
+    def gu_arrivals(k):
+        rows = rows_of(k, x)
+        return [
+            remote(WG.at[1, rows], WG.at[1, rows], y_send.at[3 + k], y_recv.at[3 + k], y_peer),
+            remote(WU.at[1, rows], WU.at[1, rows], y_send.at[3 + NK + k], y_recv.at[3 + NK + k], y_peer),
+        ]
+
+    def gu_across(k, which):
+        rows = rows_of(k, which)
+        return [
+            remote(WG.at[1, rows], WG.at[1, rows], x_send.at[1 + k], x_recv.at[1 + k], x_peer),
+            remote(WU.at[1, rows], WU.at[1, rows], x_send.at[1 + NK + k], x_recv.at[1 + NK + k], x_peer),
+        ]
+
+    def down_across(which):
+        half = pl.ds(pl.multiple_of(which * (H // 2), H // 2), H // 2)
+        return remote(WD.at[1, half], WD.at[1, half], x_send.at[0], x_recv.at[0], x_peer)
+
+    for n in range(3):
+        y_copy(n).start()
+
+    def start_gu(k, _):
+        for copy in gu_copies(k):
+            copy.start()
+        return 0
+
+    lax.fori_loop(0, NK, start_gu, 0)
+
+    sib_copy(0, z, x_hbm).start()
+    local = [
+        pltpu.make_async_copy(x_hbm, chunk(z), loc_sem.at[0]),
+        pltpu.make_async_copy(down_hbm, WD.at[0], loc_sem.at[1]),
+        pltpu.make_async_copy(gate_hbm, WG.at[0], loc_sem.at[2]),
+        pltpu.make_async_copy(up_hbm, WU.at[0], loc_sem.at[3]),
+        pltpu.make_async_copy(sg_hbm.at[:, :, y], SG.at[0], loc_sem.at[4]),
+        pltpu.make_async_copy(su_hbm.at[:, :, y], SU.at[0], loc_sem.at[5]),
+    ]
+    for copy in local:
+        copy.start()
+
+    lane = lax.broadcasted_iota(jnp.int32, (T, T), 1)
+    row = lax.broadcasted_iota(jnp.int32, (T, T), 0)
+    ids = ids_ref[...]
+    scores = scores_ref[...]
+    hit0 = lane == ids[:, 0:1]
+    hit1 = lane == ids[:, 1:2]
+    hits = jnp.where(hit0 | hit1, 1.0, 0.0)
+    earlier = jnp.where(lane < row, 1.0, 0.0).astype(BF16)
+    slots = jnp.where(hits > 0.5, dot(earlier, hits.astype(BF16), NN), -1.0)
+    factor = route_scale / (scores[:, 0:1] + scores[:, 1:2])
+    weights = jnp.where(lane == ids[:, 0:1] + 4, factor * scores[:, 0:1], 0.0)
+    weights = jnp.where(lane == ids[:, 1:2] + 4, factor * scores[:, 1:2], weights)
+    META[0] = jnp.transpose(jnp.where(lane < 4, slots, weights))[0:8]
+    for o in range(1, 8):
+        remote(META.at[0], META.at[o], meta_send.at[o], meta_recv.at[o], column(o)).start()
+
+    def take_up(d):
+        @pl.when(z - d >= 0)
+        def _():
+            up_arrival(d).wait_recv()
+            if d < ZS - 1:
+                @pl.when(z + 1 <= ZS - 1)
+                def _():
+                    up_copy(d, chunk(z - d)).start()
+            sib_copy(d, z - d, chunk(z - d)).start()
+
+    def take_down(d):
+        @pl.when(z + d <= ZS - 1)
+        def _():
+            down_arrival(d).wait_recv()
+            if d < ZS - 1:
+                @pl.when(z - 1 >= 0)
+                def _():
+                    down_copy(d, chunk(z + d)).start()
+            sib_copy(3 + d, z + d, chunk(z + d)).start()
+
+    def pass_gu(k):
+        for copy in gu_arrivals(k):
+            copy.wait_recv()
+        for copy in gu_across(k, x):
+            copy.start()
+
+    take_up(1)
+    take_down(1)
+    y_arrival(0).wait_recv()
+    down_across(x).start()
+    take_up(2)
+    take_down(2)
+    ready = 4
+    lax.fori_loop(0, ready, lambda k, _: (pass_gu(k), 0)[1], 0)
+    take_up(3)
+    take_down(3)
+    for copy in local:
+        copy.wait()
+    y_arrival(1).wait_recv()
+    y_arrival(2).wait_recv()
+    down_across(1 - x).wait_recv()
+    for o in range(1, 8):
+        remote(META.at[o], META.at[o], meta_send.at[o], meta_recv.at[o], column(o)).wait_recv()
+    sib_arrival(0, z).wait_recv()
+    for d in range(1, ZS):
+        @pl.when(z - d >= 0)
+        def _():
+            sib_arrival(d, z - d).wait_recv()
+
+        @pl.when(z + d <= ZS - 1)
+        def _():
+            sib_arrival(3 + d, z + d).wait_recv()
+
+    slot_lane = lax.broadcasted_iota(jnp.int32, (T, CAP), 1).astype(F32)
+    row8 = lax.broadcasted_iota(jnp.int32, (8, T), 0)
+    ones = jnp.ones((8, H), BF16)
+
+    def hidden(zz, _):
+        hs = [dot(X[zz], WD[b], NT) for b in range(2)]
+        for cc in range(2):
+            o = (me - (zz * 2 + cc) + 8) % 8
+            meta = jnp.transpose(jnp.concatenate([META[o], jnp.zeros((T - 8, T), F32)], axis=0))
+            slot = jnp.sum(jnp.where(lane == expert, meta, 0.0), axis=1, keepdims=True)
+            weight = jnp.sum(jnp.where(lane == expert + 4, meta, 0.0), axis=1, keepdims=True)
+            pick = jnp.where(slot == slot_lane, 1.0, 0.0).astype(BF16)
+            total = jnp.zeros((8, T), F32)
+            for b in range(2):
+                h = hs[b][cc * T:(cc + 1) * T]
+                g = dot(pick, SG[b, cc, zz], NN)
+                u = dot(pick, SU[b, cc, zz], NN)
+                sig = jax.nn.sigmoid(g)
+                act = g * sig
+                prod = h * act * u
+                high = prod.astype(BF16)
+                low = (prod - high.astype(F32)).astype(BF16)
+                total = total + dot(ones, high, NT) + dot(ones, low, NT)
+                scaled = h * weight
+                rows = pl.ds(pl.multiple_of(zz * T, T), T)
+                DGU[cc, rows, b * 2 * H:b * 2 * H + H] = (
+                    scaled * u * sig * (1.0 + g * (1.0 - sig))
+                ).astype(BF16)
+                DGU[cc, rows, b * 2 * H + H:(b + 1) * 2 * H] = (scaled * act).astype(BF16)
+            PRS[zz * 2 + cc] = jnp.where(row8 == expert, total, 0.0)
+        return 0
+
+    lax.fori_loop(0, ZS, hidden, 0)
+    for o in range(1, 8):
+        remote(PRS.at[(me + o) % 8], PRR.at[o], pr_send.at[o], pr_recv.at[o], column(o)).start()
+
+    def share(k):
+        return remote(SS.at[k], SR.at[k], cs_send.at[k], cs_recv.at[k], sibling)
+
+    def up_out(k, d):
+        return remote(UPOUT.at[d - 1, k], UPIN.at[d - 1, k], u_send.at[d - 1, k], u_recv.at[d - 1, k], above)
+
+    def down_out(k, d):
+        return remote(DNOUT.at[d - 1, k], DNIN.at[d - 1, k], d_send.at[d - 1, k], d_recv.at[d - 1, k], below)
+
+    def up_in(k, d):
+        return remote(UPIN.at[d, k], UPIN.at[d, k], u_send.at[d, k], u_recv.at[d, k], below)
+
+    def down_in(k, d):
+        return remote(DNIN.at[d, k], DNIN.at[d, k], d_send.at[d, k], d_recv.at[d, k], above)
+
+    def partial(k, cc):
+        rows = pl.ds(pl.multiple_of(k * WIDE, WIDE), WIDE)
+        acc = dot(DGU[cc, :, 0:H], WG[0, rows], NT)
+        acc = acc + dot(DGU[cc, :, H:2 * H], WU[0, rows], NT)
+        acc = acc + dot(DGU[cc, :, 2 * H:3 * H], WG[1, rows], NT)
+        return acc + dot(DGU[cc, :, 3 * H:4 * H], WU[1, rows], NT)
+
+    def compute(k):
+        for copy in gu_across(k, 1 - x):
+            copy.wait_recv()
+        SS[k] = partial(k, 1 - c).reshape(ZS, T, WIDE).astype(BF16)
+        share(k).start()
+        QF[k % 4] = partial(k, c).reshape(ZS, T, WIDE)
+
+    def mine(k, zz):
+        return QF[k % 4, zz] + SR[k, zz].astype(F32)
+
+    def chain(k):
+        share(k).wait_recv()
+        for d in (3, 2, 1):
+            @pl.when(z + d <= ZS - 1)
+            def _():
+                @pl.when(z == 0)
+                def _():
+                    UPOUT[d - 1, k] = mine(k, z + d).astype(BF16)
+                if d < 3:
+                    @pl.when(z > 0)
+                    def _():
+                        up_in(k, d).wait_recv()
+                        UPOUT[d - 1, k] = (mine(k, z + d) + UPIN[d, k].astype(F32)).astype(BF16)
+                up_out(k, d).start()
+
+            @pl.when(z - d >= 0)
+            def _():
+                @pl.when(z == ZS - 1)
+                def _():
+                    DNOUT[d - 1, k] = mine(k, z - d).astype(BF16)
+                if d < 3:
+                    @pl.when(z < ZS - 1)
+                    def _():
+                        down_in(k, d).wait_recv()
+                        DNOUT[d - 1, k] = (mine(k, z - d) + DNIN[d, k].astype(F32)).astype(BF16)
+                down_out(k, d).start()
+
+    def final(k):
+        FIN[...] = mine(k, z)
+
+        @pl.when(z > 0)
+        def _():
+            up_in(k, 0).wait_recv()
+            FIN[...] += UPIN[0, k].astype(F32)
+
+        @pl.when(z < ZS - 1)
+        def _():
+            down_in(k, 0).wait_recv()
+            FIN[...] += DNIN[0, k].astype(F32)
+
+        out_ref[:, pl.ds(pl.multiple_of(k * WIDE, WIDE), WIDE)] = FIN[...].astype(BF16)
+
+    def step(i, _):
+        @pl.when(i + ready < NK)
+        def _():
+            pass_gu(i + ready)
+
+        @pl.when(i < NK)
+        def _():
+            compute(i)
+
+        @pl.when((i >= 1) & (i <= NK))
+        def _():
+            chain(i - 1)
+
+        @pl.when(i >= 2)
+        def _():
+            final(i - 2)
+
+        return 0
+
+    lax.fori_loop(0, NK + 2, step, 0)
+
+    total = PRS[me]
+    for o in range(1, 8):
+        remote(PRR.at[o], PRR.at[o], pr_send.at[o], pr_recv.at[o], column(o)).wait_recv()
+        total = total + PRR[o]
+    prod_ref[...] = total
+
+    for o in range(1, 8):
+        remote(META.at[0], META.at[o], meta_send.at[o], meta_recv.at[o], column(o)).wait_send()
+        remote(PRS.at[(me + o) % 8], PRR.at[o], pr_send.at[o], pr_recv.at[o], column(o)).wait_send()
+    for n in range(3):
+        y_copy(n).wait_send()
+    down_across(x).wait_send()
+    sib_copy(0, z, x_hbm).wait_send()
+
+    @pl.when(z < ZS - 1)
+    def _():
+        up_copy(0, x_hbm).wait_send()
+
+    @pl.when(z > 0)
+    def _():
+        down_copy(0, x_hbm).wait_send()
+
+    for d in range(1, ZS):
+        @pl.when(z - d >= 0)
+        def _():
+            sib_copy(d, z - d, chunk(z - d)).wait_send()
+            if d < ZS - 1:
+                @pl.when(z + 1 <= ZS - 1)
+                def _():
+                    up_copy(d, chunk(z - d)).wait_send()
+
+        @pl.when(z + d <= ZS - 1)
+        def _():
+            sib_copy(3 + d, z + d, chunk(z + d)).wait_send()
+            if d < ZS - 1:
+                @pl.when(z - 1 >= 0)
+                def _():
+                    down_copy(d, chunk(z + d)).wait_send()
+
+    def finish(k, _):
+        for copy in gu_copies(k) + gu_across(k, x):
+            copy.wait_send()
+        share(k).wait_send()
+        for d in (3, 2, 1):
+            @pl.when(z + d <= ZS - 1)
+            def _():
+                up_out(k, d).wait_send()
+
+            @pl.when(z - d >= 0)
+            def _():
+                down_out(k, d).wait_send()
+        return 0
+
+    lax.fori_loop(0, NK, finish, 0)
+
+
+def fused_on_device(
+    grad_out, expert_ids, scores, gate_weight, up_weight, down_weight, saved_gate, saved_up
+):
+    T, D = grad_out.shape
+    H = gate_weight.shape[2]
+    cap = saved_gate.shape[1] // 16
+    NK = D // WIDE
+    dma = pltpu.SemaphoreType.DMA
+    vmem = pl.BlockSpec(memory_space=pltpu.VMEM)
+    hbm = pl.BlockSpec(memory_space=pl.ANY)
+    grad_in, products = pl.pallas_call(
+        fused,
+        out_shape=(jax.ShapeDtypeStruct((T, D), BF16), jax.ShapeDtypeStruct((8, T), F32)),
+        in_specs=[vmem, vmem] + [hbm] * 6,
+        out_specs=(vmem, vmem),
+        scratch_shapes=[
+            pltpu.VMEM((ZS, 2 * T, D), BF16),
+            pltpu.VMEM((2, H, D), BF16),
+            pltpu.VMEM((2, D, H), BF16),
+            pltpu.VMEM((2, D, H), BF16),
+            pltpu.VMEM((2, 2, ZS, cap, H), BF16),
+            pltpu.VMEM((2, 2, ZS, cap, H), BF16),
+            pltpu.VMEM((8, 8, T), F32),
+            pltpu.VMEM((2, ZS * T, 4 * H), BF16),
+            pltpu.VMEM((4, ZS, T, WIDE), F32),
+            pltpu.VMEM((NK, ZS, T, WIDE), BF16),
+            pltpu.VMEM((NK, ZS, T, WIDE), BF16),
+            pltpu.VMEM((3, NK, T, WIDE), BF16),
+            pltpu.VMEM((3, NK, T, WIDE), BF16),
+            pltpu.VMEM((3, NK, T, WIDE), BF16),
+            pltpu.VMEM((3, NK, T, WIDE), BF16),
+            pltpu.VMEM((T, WIDE), F32),
+            pltpu.VMEM((8, 8, T), F32),
+            pltpu.VMEM((8, 8, T), F32),
+            dma((6,)),
+            dma((3 + 2 * NK,)), dma((3 + 2 * NK,)),
+            dma((1 + 2 * NK,)), dma((1 + 2 * NK,)),
+            dma((2, 3)), dma((2, 3)),
+            dma((7,)), dma((7,)),
+            dma((8,)), dma((8,)),
+            dma((8,)), dma((8,)),
+            dma((NK,)), dma((NK,)),
+            dma((3, NK)), dma((3, NK)),
+            dma((3, NK)), dma((3, NK)),
+        ],
+        compiler_params=pltpu.CompilerParams(
+            collective_id=0, has_side_effects=True, vmem_limit_bytes=62 * 1024 * 1024
+        ),
+    )(
+        expert_ids, scores, grad_out, gate_weight[0], up_weight[0], down_weight[0],
+        saved_gate.reshape(2, ZS, 2, cap, H), saved_up.reshape(2, ZS, 2, cap, H),
+    )
+    hit = expert_ids[:, :, None] == jnp.arange(8, dtype=jnp.int32)[None, None, :]
+    picked = jnp.sum(jnp.where(hit, products.T[:, None, :], 0.0), axis=2)
+    total = jnp.sum(scores, axis=1, keepdims=True)
+    centred = picked - jnp.sum(picked * scores, axis=1, keepdims=True) / total
+    grad_logit = route_scale / total * centred * scores * (1.0 - scores)
+    return grad_in, grad_logit
+
+
 def solution(mesh):
     in_specs = (
         P(("parts", "node", "rank"), None),
@@ -134,6 +602,7 @@
         P(("parts", "node", "rank"), None, None),
     )
     out_specs = (P(("parts", "node", "rank"), None), P(("parts", "node", "rank"), None))
+    small = (mesh.shape["parts"], mesh.shape["node"], mesh.shape["rank"]) == (2, 2, 8)
     return jax.shard_map(
-        on_device, mesh=mesh, in_specs=in_specs, out_specs=out_specs, check_vma=False
-    )
+        fused_on_device if small else on_device, mesh=mesh, in_specs=in_specs, out_specs=out_specs, check_vma=False
+    )

time: 670 us -> 156 us (0.23)
  waiting for transfers between devices: 512 us -> 0 us
  Pallas kernels: 0 us -> 149 us
  local copies, waits for them, and re-layouts: 68.3 us -> 4.99 us
  starting transfers between devices: 35 us -> 0 us
  matrix products: 28.4 us -> 0 us
  other arithmetic: 24.1 us -> 1.3 us
    all_to_all x3 -> x0, waiting for transfers between devices: 275 us -> none  [the longest x1 218 us: on_device(): lax.all_to_all(outgoing, ('node', 'rank'), split_axis=1, concat_axis=1, t...]
    ppermute x4 -> x0, waiting for transfers between devices: 237 us -> none  [from_partner(): return lax.ppermute(block, axis, route)]
    pallas_call x0 -> x1, Pallas kernels: none -> 149 us  [fused_on_device(): pl.pallas_call(fused, out_shape=(jax.ShapeDtypeStruct((T, D), BF16), jax....]
    dot_general x3 -> x0, matrix products: 28.4 us -> none  [the longest x1 15.6 us: on_device(): lax.dot_general(d_up, up_weight[0], contract, preferred_element_type=jnp....]
    all_to_all x3 -> x0, starting transfers between devices: 18.5 us -> none  [the longest x1 7.57 us: on_device(): lax.all_to_all(outgoing, ('node', 'rank'), split_axis=1, concat_axis=1, t...]
    ppermute x4 -> x0, starting transfers between devices: 16.5 us -> none  [from_partner(): return lax.ppermute(block, axis, route)]
    broadcast_in_dim x3 -> x0, local copies, waits for them, and re-layouts: 14.1 us -> none  [the longest x2 10.7 us: on_device(): jnp.broadcast_to(buffered, (SPLIT, expert_count, SPLIT, quarter, feature_...]
    convert_element_type x8 -> x0, local copies, waits for them, and re-layouts: 13.2 us -> none  [the longest x4 7.61 us: arranged(): return ordered.reshape(-1, hidden_width).astype(jnp.float32)]
  transfers between devices with their start and end apart: 7 -> 0, of which waited for: 5 -> 0; matrix products, arithmetic and copies ran while one was open for 3% -> 0% of each run, Pallas kernels for 0% -> 0%
where the time goes in v2:
time: 156 us
  Pallas kernels  149 us (96%)
  local copies, waits for them, and re-layouts  4.99 us (3%)
    pallas_call x1, Pallas kernels, fused_on_device(): pl.pallas_call(fused, out_shape=(jax.ShapeDtypeStruct((T, D), BF16), jax....  149 us
    unnamed x7, local copies, waits for them, and re-layouts  4.99 us

profile of v2, /device:TPU:0, one launch (start us, length us, event | category | flops | bytes accessed | tf_op | source)
XLA Modules:
  0.0 155.8 jit_solution(1583355423233301487)
XLA Ops:
  0.6 1.4 copy.14.ids_ref
  2.0 1.4 copy.15.scores_ref
  3.4 0.0 copy-start.1
  3.5 0.0 copy-start
  3.5 148.9 %shard_map.95 = (bf16[128,3584]{1,0:T(8,128)(2,1)}, f32[8,128]{1,0:T(8,128)}) custom-call(s32[128,2]{1,0:T(8,128)} %copy.14.ids_ref, f32[128,2]{1,0:T(8,128)} %copy.15.scores_ref, bf16[128,3584]{1,0:T(8,128)(2,1)} %x_hbm.1, bf16[3584,256]{1,0:T(8,128)(2,1)} %bitcast.6, bf16[3584,256]{1,0:T(8,128)(2,1)} %bitcast.7, bf16[256,3584]{1,0:T(8,128)(2,1)} %bitcast.8, ...), custom_call_target="tpu_custom_call" | custom-call | tf_op jit(solution)/shard_map/pallas_call | solution.py:543
  152.3 0.0 copy-done.1
  152.4 0.7 select_reduce_fusion
  153.0 0.0 copy-done
  153.1 0.6 subtract_multiply_fusion
  153.7 2.2 %copy.17 = bf16[128,3584]{1,0:T(8,128)(2,1)} copy(bf16[128,3584]{1,0:T(8,128)(2,1)} %get-tuple-element.12) | data formatting | bytes 1835008
  (2 shorter events, 0.0 us)
Async XLA Ops:
  3.4 148.9 %copy-start.1 = (s32[128,2]{0,1:T(2,128)S(1)}, s32[128,2]{0,1:T(2,128)}, u32[]{:S(2)}) copy-start(s32[128,2]{0,1:T(2,128)} %param.9) | copy-start | bytes 3076
  3.5 149.6 %copy-start = (f32[128,2]{0,1:T(2,128)S(1)}, f32[128,2]{0,1:T(2,128)}, u32[]{:S(2)}) copy-start(f32[128,2]{0,1:T(2,128)} %param.10) | copy-start | bytes 3076

commit v3 on v2

--- a/solution.py
+++ b/solution.py
@@ -208,59 +208,55 @@
     def _():
         down_copy(0, x_hbm).start()
 
-    def piece(n):
-        if n == 0:
-            half = pl.ds(pl.multiple_of(x * (H // 2), H // 2), H // 2)
-            return down_hbm.at[half], WD.at[1, half]
-        if n == 1:
-            return sg_hbm.at[:, :, 1 - y], SG.at[1]
-        return su_hbm.at[:, :, 1 - y], SU.at[1]
-
-    def y_copy(n):
-        src, dst = piece(n)
-        return remote(src, dst, y_send.at[n], y_recv.at[n], y_peer)
-
-    def y_arrival(n):
-        dst = piece(n)[1]
-        return remote(dst, dst, y_send.at[n], y_recv.at[n], y_peer)
-
-    def rows_of(k, which):
+    def job(s):
+        order = ((1, 2, 3, 0), (0, 2, 3, 1), (3, 1, 0, 2), (2, 1, 0, 3))
+        return jnp.where(
+            z == 0, order[0][s], jnp.where(z == 1, order[1][s], jnp.where(z == 2, order[2][s], order[3][s]))
+        )
+
+    EIGHTH = H // 8
+
+    def down_rows(n, which):
+        return pl.ds(pl.multiple_of(which * (H // 2) + n * EIGHTH, EIGHTH), EIGHTH)
+
+    def gu_rows(k, which):
         return pl.ds(pl.multiple_of(k * WIDE + which * (WIDE // 2), WIDE // 2), WIDE // 2)
 
-    def gu_copies(k):
-        rows = rows_of(k, x)
+    def refs_down(n, which):
+        rows = down_rows(n, which)
+        return [(down_hbm.at[rows], WD.at[1, rows], n)]
+
+    def refs_gu(k, which):
+        rows = gu_rows(k, which)
+        return [(gate_hbm.at[rows], WG.at[1, rows], 4 + k), (up_hbm.at[rows], WU.at[1, rows], 4 + NK + k)]
+
+    def refs_saved(s):
+        zz = job(s)
+        base = 4 + 2 * NK + 2 * s
         return [
-            remote(gate_hbm.at[rows], WG.at[1, rows], y_send.at[3 + k], y_recv.at[3 + k], y_peer),
-            remote(up_hbm.at[rows], WU.at[1, rows], y_send.at[3 + NK + k], y_recv.at[3 + NK + k], y_peer),
+            (sg_hbm.at[:, zz, 1 - y], SG.at[1, :, zz], base),
+            (su_hbm.at[:, zz, 1 - y], SU.at[1, :, zz], base + 1),
         ]
 
-    def gu_arrivals(k):
-        rows = rows_of(k, x)
-        return [
-            remote(WG.at[1, rows], WG.at[1, rows], y_send.at[3 + k], y_recv.at[3 + k], y_peer),
-            remote(WU.at[1, rows], WU.at[1, rows], y_send.at[3 + NK + k], y_recv.at[3 + NK + k], y_peer),
-        ]
-
-    def gu_across(k, which):
-        rows = rows_of(k, which)
-        return [
-            remote(WG.at[1, rows], WG.at[1, rows], x_send.at[1 + k], x_recv.at[1 + k], x_peer),
-            remote(WU.at[1, rows], WU.at[1, rows], x_send.at[1 + NK + k], x_recv.at[1 + NK + k], x_peer),
-        ]
-
-    def down_across(which):
-        half = pl.ds(pl.multiple_of(which * (H // 2), H // 2), H // 2)
-        return remote(WD.at[1, half], WD.at[1, half], x_send.at[0], x_recv.at[0], x_peer)
-
-    for n in range(3):
-        y_copy(n).start()
-
-    def start_gu(k, _):
-        for copy in gu_copies(k):
+    def over_y(refs):
+        return [remote(src, dst, y_send.at[n], y_recv.at[n], y_peer) for src, dst, n in refs]
+
+    def from_y(refs):
+        return [remote(dst, dst, y_send.at[n], y_recv.at[n], y_peer) for _, dst, n in refs]
+
+    def over_x(refs):
+        return [remote(dst, dst, x_send.at[n], x_recv.at[n], x_peer) for _, dst, n in refs]
+
+    def begin(copies):
+        for copy in copies:
             copy.start()
-        return 0
-
-    lax.fori_loop(0, NK, start_gu, 0)
+
+    def arrive(copies):
+        for copy in copies:
+            copy.wait_recv()
+
+    for n in range(4):
+        begin(over_y(refs_down(n, x)))
 
     sib_copy(0, z, x_hbm).start()
     local = [
@@ -310,44 +306,16 @@
                     down_copy(d, chunk(z + d)).start()
             sib_copy(3 + d, z + d, chunk(z + d)).start()
 
-    def pass_gu(k):
-        for copy in gu_arrivals(k):
-            copy.wait_recv()
-        for copy in gu_across(k, x):
-            copy.start()
-
-    take_up(1)
-    take_down(1)
-    y_arrival(0).wait_recv()
-    down_across(x).start()
-    take_up(2)
-    take_down(2)
-    ready = 4
-    lax.fori_loop(0, ready, lambda k, _: (pass_gu(k), 0)[1], 0)
-    take_up(3)
-    take_down(3)
-    for copy in local:
-        copy.wait()
-    y_arrival(1).wait_recv()
-    y_arrival(2).wait_recv()
-    down_across(1 - x).wait_recv()
-    for o in range(1, 8):
-        remote(META.at[o], META.at[o], meta_send.at[o], meta_recv.at[o], column(o)).wait_recv()
-    sib_arrival(0, z).wait_recv()
-    for d in range(1, ZS):
-        @pl.when(z - d >= 0)
-        def _():
-            sib_arrival(d, z - d).wait_recv()
-
-        @pl.when(z + d <= ZS - 1)
-        def _():
-            sib_arrival(3 + d, z + d).wait_recv()
+    def pass_on(refs):
+        arrive(from_y(refs))
+        begin(over_x(refs))
 
     slot_lane = lax.broadcasted_iota(jnp.int32, (T, CAP), 1).astype(F32)
     row8 = lax.broadcasted_iota(jnp.int32, (8, T), 0)
     ones = jnp.ones((8, H), BF16)
 
-    def hidden(zz, _):
+    def hidden(s):
+        zz = job(s)
         hs = [dot(X[zz], WD[b], NT) for b in range(2)]
         for cc in range(2):
             o = (me - (zz * 2 + cc) + 8) % 8
@@ -356,6 +324,7 @@
             weight = jnp.sum(jnp.where(lane == expert + 4, meta, 0.0), axis=1, keepdims=True)
             pick = jnp.where(slot == slot_lane, 1.0, 0.0).astype(BF16)
             total = jnp.zeros((8, T), F32)
+            rows = pl.ds(pl.multiple_of(((cc + c) % 2) * T, T), T)
             for b in range(2):
                 h = hs[b][cc * T:(cc + 1) * T]
                 g = dot(pick, SG[b, cc, zz], NN)
@@ -367,112 +336,228 @@
                 low = (prod - high.astype(F32)).astype(BF16)
                 total = total + dot(ones, high, NT) + dot(ones, low, NT)
                 scaled = h * weight
-                rows = pl.ds(pl.multiple_of(zz * T, T), T)
-                DGU[cc, rows, b * 2 * H:b * 2 * H + H] = (
+                DGU[s, rows, b * 2 * H:b * 2 * H + H] = (
                     scaled * u * sig * (1.0 + g * (1.0 - sig))
                 ).astype(BF16)
-                DGU[cc, rows, b * 2 * H + H:(b + 1) * 2 * H] = (scaled * act).astype(BF16)
+                DGU[s, rows, b * 2 * H + H:(b + 1) * 2 * H] = (scaled * act).astype(BF16)
             PRS[zz * 2 + cc] = jnp.where(row8 == expert, total, 0.0)
+
+    def share(s, k):
+        return remote(SS.at[s, k], SR.at[s, k], cs_send.at[s, k], cs_recv.at[s, k], sibling)
+
+    def up_out(s, k):
+        return remote(UPOUT.at[s, k], UPIN.at[s, k], u_send.at[s, k], u_recv.at[s, k], above)
+
+    def down_out(s, k):
+        return remote(DNOUT.at[s, k], DNIN.at[s, k], d_send.at[s, k], d_recv.at[s, k], below)
+
+    def up_in(s, k):
+        return remote(UPIN.at[s, k], UPIN.at[s, k], u_send.at[s, k], u_recv.at[s, k], below)
+
+    def down_in(s, k):
+        return remote(DNIN.at[s, k], DNIN.at[s, k], d_send.at[s, k], d_recv.at[s, k], above)
+
+    def compute(s, k):
+        rows = pl.ds(pl.multiple_of(k * WIDE, WIDE), WIDE)
+        acc = dot(DGU[s, :, 0:H], WG[0, rows], NT)
+        acc = acc + dot(DGU[s, :, H:2 * H], WU[0, rows], NT)
+        acc = acc + dot(DGU[s, :, 2 * H:3 * H], WG[1, rows], NT)
+        acc = acc + dot(DGU[s, :, 3 * H:4 * H], WU[1, rows], NT)
+        SS[s, k] = acc[T:2 * T].astype(BF16)
+        share(s, k).start()
+        QF[s, k] = acc[0:T]
+
+    def mine(s, k):
+        return QF[s, k] + SR[s, k].astype(F32)
+
+    def send_up(t, k, s):
+        @pl.when(z == 0)
+        def _():
+            UPOUT[t, k] = mine(s, k).astype(BF16)
+
+        @pl.when(z > 0)
+        def _():
+            up_in(t, k).wait_recv()
+            UPOUT[t, k] = (mine(s, k) + UPIN[t, k].astype(F32)).astype(BF16)
+
+        up_out(t, k).start()
+
+    def send_down(t, k, s):
+        @pl.when(z == ZS - 1)
+        def _():
+            DNOUT[t, k] = mine(s, k).astype(BF16)
+
+        @pl.when(z < ZS - 1)
+        def _():
+            down_in(t, k).wait_recv()
+            DNOUT[t, k] = (mine(s, k) + DNIN[t, k].astype(F32)).astype(BF16)
+
+        down_out(t, k).start()
+
+    def chain(t, k):
+        share(t, k).wait_recv()
+        if t == 0:
+            @pl.when(z == 0)
+            def _():
+                send_up(0, k, 0)
+
+            @pl.when(z == ZS - 1)
+            def _():
+                send_down(0, k, 0)
+        elif t == 1:
+            @pl.when(z <= 1)
+            def _():
+                send_up(1, k, 1)
+
+            @pl.when(z >= 2)
+            def _():
+                send_down(1, k, 1)
+        else:
+            @pl.when(z <= 1)
+            def _():
+                send_up(2, k, 2)
+
+            @pl.when(z >= 2)
+            def _():
+                send_down(2, k, 2)
+
+            @pl.when(z == 1)
+            def _():
+                send_down(2, k, 0)
+
+            @pl.when(z == 2)
+            def _():
+                send_up(2, k, 0)
+
+    def final(k):
+        share(3, k).wait_recv()
+        FIN[...] = mine(3, k)
+
+        @pl.when(z > 0)
+        def _():
+            t = jnp.maximum(z - 1, 0)
+            up_in(t, k).wait_recv()
+            FIN[...] += UPIN[t, k].astype(F32)
+
+        @pl.when(z < ZS - 1)
+        def _():
+            t = jnp.maximum(2 - z, 0)
+            down_in(t, k).wait_recv()
+            FIN[...] += DNIN[t, k].astype(F32)
+
+        out_ref[:, pl.ds(pl.multiple_of(k * WIDE, WIDE), WIDE)] = FIN[...].astype(BF16)
+
+    def chunk_ready(d):
+        @pl.when(z - d >= 0)
+        def _():
+            sib_arrival(d, z - d).wait_recv()
+
+        @pl.when(z + d <= ZS - 1)
+        def _():
+            sib_arrival(3 + d, z + d).wait_recv()
+
+    pass_on(refs_down(0, x))
+    begin(over_y(refs_saved(0)))
+    pass_on(refs_down(1, x))
+    begin(over_y(refs_gu(0, x)))
+    pass_on(refs_down(2, x))
+    begin(over_y(refs_gu(1, x)))
+    take_up(1)
+    take_down(1)
+    pass_on(refs_down(3, x))
+    for copy in local:
+        copy.wait()
+    for o in range(1, 8):
+        remote(META.at[o], META.at[o], meta_send.at[o], meta_recv.at[o], column(o)).wait_recv()
+    arrive(from_y(refs_saved(0)))
+    begin(over_y(refs_gu(2, x)))
+    for n in range(4):
+        arrive(over_x(refs_down(n, 1 - x)))
+    chunk_ready(1)
+    hidden(0)
+
+    def round0(i, _):
+        @pl.when(i < NK)
+        def _():
+            pass_on(refs_gu(i, x))
+
+        @pl.when(i + 3 < NK)
+        def _():
+            begin(over_y(refs_gu(i + 3, x)))
+
+        for s in (1, 2, 3):
+            @pl.when(i == NK - 4 + s)
+            def _():
+                begin(over_y(refs_saved(s)))
+
+        @pl.when(i == 2)
+        def _():
+            take_up(2)
+            take_down(2)
+
+        @pl.when(i >= 1)
+        def _():
+            arrive(over_x(refs_gu(i - 1, 1 - x)))
+            compute(0, i - 1)
+
+        @pl.when(i >= 2)
+        def _():
+            chain(0, i - 2)
+
         return 0
 
-    lax.fori_loop(0, ZS, hidden, 0)
+    lax.fori_loop(0, NK + 2 - 1, round0, 0)
+    chain(0, NK - 1)
+    arrive(from_y(refs_saved(1)))
+    chunk_ready(2)
+    hidden(1)
+
+    def round1(i, _):
+        @pl.when(i < NK)
+        def _():
+            compute(1, i)
+
+        @pl.when(i >= 1)
+        def _():
+            chain(1, i - 1)
+
+        @pl.when(i == 0)
+        def _():
+            take_up(3)
+            take_down(3)
+
+        return 0
+
+    lax.fori_loop(0, NK + 1, round1, 0)
+    arrive(from_y(refs_saved(2)))
+    chunk_ready(3)
+    hidden(2)
+    arrive(from_y(refs_saved(3)))
+    sib_arrival(0, z).wait_recv()
+
+    def round2(i, _):
+        @pl.when(i < NK)
+        def _():
+            compute(2, i)
+
+        @pl.when(i >= 1)
+        def _():
+            chain(2, i - 1)
+
+        @pl.when(i == 0)
+        def _():
+            hidden(3)
+
+        @pl.when(i < NK)
+        def _():
+            compute(3, i)
+
+        return 0
+
+    lax.fori_loop(0, NK + 1, round2, 0)
     for o in range(1, 8):
         remote(PRS.at[(me + o) % 8], PRR.at[o], pr_send.at[o], pr_recv.at[o], column(o)).start()
-
-    def share(k):
-        return remote(SS.at[k], SR.at[k], cs_send.at[k], cs_recv.at[k], sibling)
-
-    def up_out(k, d):
-        return remote(UPOUT.at[d - 1, k], UPIN.at[d - 1, k], u_send.at[d - 1, k], u_recv.at[d - 1, k], above)
-
-    def down_out(k, d):
-        return remote(DNOUT.at[d - 1, k], DNIN.at[d - 1, k], d_send.at[d - 1, k], d_recv.at[d - 1, k], below)
-
-    def up_in(k, d):
-        return remote(UPIN.at[d, k], UPIN.at[d, k], u_send.at[d, k], u_recv.at[d, k], below)
-
-    def down_in(k, d):
-        return remote(DNIN.at[d, k], DNIN.at[d, k], d_send.at[d, k], d_recv.at[d, k], above)
-
-    def partial(k, cc):
-        rows = pl.ds(pl.multiple_of(k * WIDE, WIDE), WIDE)
-        acc = dot(DGU[cc, :, 0:H], WG[0, rows], NT)
-        acc = acc + dot(DGU[cc, :, H:2 * H], WU[0, rows], NT)
-        acc = acc + dot(DGU[cc, :, 2 * H:3 * H], WG[1, rows], NT)
-        return acc + dot(DGU[cc, :, 3 * H:4 * H], WU[1, rows], NT)
-
-    def compute(k):
-        for copy in gu_across(k, 1 - x):
-            copy.wait_recv()
-        SS[k] = partial(k, 1 - c).reshape(ZS, T, WIDE).astype(BF16)
-        share(k).start()
-        QF[k % 4] = partial(k, c).reshape(ZS, T, WIDE)
-
-    def mine(k, zz):
-        return QF[k % 4, zz] + SR[k, zz].astype(F32)
-
-    def chain(k):
-        share(k).wait_recv()
-        for d in (3, 2, 1):
-            @pl.when(z + d <= ZS - 1)
-            def _():
-                @pl.when(z == 0)
-                def _():
-                    UPOUT[d - 1, k] = mine(k, z + d).astype(BF16)
-                if d < 3:
-                    @pl.when(z > 0)
-                    def _():
-                        up_in(k, d).wait_recv()
-                        UPOUT[d - 1, k] = (mine(k, z + d) + UPIN[d, k].astype(F32)).astype(BF16)
-                up_out(k, d).start()
-
-            @pl.when(z - d >= 0)
-            def _():
-                @pl.when(z == ZS - 1)
-                def _():
-                    DNOUT[d - 1, k] = mine(k, z - d).astype(BF16)
-                if d < 3:
-                    @pl.when(z < ZS - 1)
-                    def _():
-                        down_in(k, d).wait_recv()
-                        DNOUT[d - 1, k] = (mine(k, z - d) + DNIN[d, k].astype(F32)).astype(BF16)
-                down_out(k, d).start()
-
-    def final(k):
-        FIN[...] = mine(k, z)
-
-        @pl.when(z > 0)
-        def _():
-            up_in(k, 0).wait_recv()
-            FIN[...] += UPIN[0, k].astype(F32)
-
-        @pl.when(z < ZS - 1)
-        def _():
-            down_in(k, 0).wait_recv()
-            FIN[...] += DNIN[0, k].astype(F32)
-
-        out_ref[:, pl.ds(pl.multiple_of(k * WIDE, WIDE), WIDE)] = FIN[...].astype(BF16)
-
-    def step(i, _):
-        @pl.when(i + ready < NK)
-        def _():
-            pass_gu(i + ready)
-
-        @pl.when(i < NK)
-        def _():
-            compute(i)
-
-        @pl.when((i >= 1) & (i <= NK))
-        def _():
-            chain(i - 1)
-
-        @pl.when(i >= 2)
-        def _():
-            final(i - 2)
-
-        return 0
-
-    lax.fori_loop(0, NK + 2, step, 0)
+    lax.fori_loop(0, NK, lambda k, _: (final(k), 0)[1], 0)
 
     total = PRS[me]
     for o in range(1, 8):
@@ -483,9 +568,9 @@
     for o in range(1, 8):
         remote(META.at[0], META.at[o], meta_send.at[o], meta_recv.at[o], column(o)).wait_send()
         remote(PRS.at[(me + o) % 8], PRR.at[o], pr_send.at[o], pr_recv.at[o], column(o)).wait_send()
-    for n in range(3):
-        y_copy(n).wait_send()
-    down_across(x).wait_send()
+    for n in range(4):
+        for copy in over_y(refs_down(n, x)) + over_x(refs_down(n, x)) + over_y(refs_saved(n)):
+            copy.wait_send()
     sib_copy(0, z, x_hbm).wait_send()
 
     @pl.when(z < ZS - 1)
@@ -514,17 +599,18 @@
                     down_copy(d, chunk(z + d)).wait_send()
 
     def finish(k, _):
-        for copy in gu_copies(k) + gu_across(k, x):
+        for copy in over_y(refs_gu(k, x)) + over_x(refs_gu(k, x)):
             copy.wait_send()
-        share(k).wait_send()
-        for d in (3, 2, 1):
-            @pl.when(z + d <= ZS - 1)
-            def _():
-                up_out(k, d).wait_send()
-
-            @pl.when(z - d >= 0)
-            def _():
-                down_out(k, d).wait_send()
+        for s in range(4):
+            share(s, k).wait_send()
+        for t in range(3):
+            @pl.when(z <= t)
+            def _():
+                up_out(t, k).wait_send()
+
+            @pl.when(z >= ZS - 1 - t)
+            def _():
+                down_out(t, k).wait_send()
         return 0
 
     lax.fori_loop(0, NK, finish, 0)
@@ -553,10 +639,10 @@
             pltpu.VMEM((2, 2, ZS, cap, H), BF16),
             pltpu.VMEM((2, 2, ZS, cap, H), BF16),
             pltpu.VMEM((8, 8, T), F32),
-            pltpu.VMEM((2, ZS * T, 4 * H), BF16),
-            pltpu.VMEM((4, ZS, T, WIDE), F32),
-            pltpu.VMEM((NK, ZS, T, WIDE), BF16),
-            pltpu.VMEM((NK, ZS, T, WIDE), BF16),
+            pltpu.VMEM((4, 2 * T, 4 * H), BF16),
+            pltpu.VMEM((4, NK, T, WIDE), F32),
+            pltpu.VMEM((4, NK, T, WIDE), BF16),
+            pltpu.VMEM((4, NK, T, WIDE), BF16),
             pltpu.VMEM((3, NK, T, WIDE), BF16),
             pltpu.VMEM((3, NK, T, WIDE), BF16),
             pltpu.VMEM((3, NK, T, WIDE), BF16),
@@ -565,13 +651,13 @@
             pltpu.VMEM((8, 8, T), F32),
             pltpu.VMEM((8, 8, T), F32),
             dma((6,)),
-            dma((3 + 2 * NK,)), dma((3 + 2 * NK,)),
-            dma((1 + 2 * NK,)), dma((1 + 2 * NK,)),
+            dma((12 + 2 * NK,)), dma((12 + 2 * NK,)),
+            dma((4 + 2 * NK,)), dma((4 + 2 * NK,)),
             dma((2, 3)), dma((2, 3)),
             dma((7,)), dma((7,)),
             dma((8,)), dma((8,)),
             dma((8,)), dma((8,)),
-            dma((NK,)), dma((NK,)),
+            dma((4, NK)), dma((4, NK)),
             dma((3, NK)), dma((3, NK)),
             dma((3, NK)), dma((3, NK)),
         ],

time: 156 us -> 165 us (1.058)
  Pallas kernels: 149 us -> 158 us
    pallas_call x1, Pallas kernels: 149 us -> 158 us  [fused_on_device(): pl.pallas_call(fused, out_shape=(jax.ShapeDtypeStruct((T, D), BF16), jax....]
where the time goes in v3:
time: 165 us
  Pallas kernels  158 us (96%)
  local copies, waits for them, and re-layouts  4.99 us (3%)
    pallas_call x1, Pallas kernels, fused_on_device(): pl.pallas_call(fused, out_shape=(jax.ShapeDtypeStruct((T, D), BF16), jax....  158 us
    unnamed x7, local copies, waits for them, and re-layouts  4.99 us

profile of v3, /device:TPU:0, one launch (start us, length us, event | category | flops | bytes accessed | tf_op | source)
XLA Modules:
  0.0 164.8 jit_solution(1389851536281574562)
XLA Ops:
  0.6 1.4 copy.14.ids_ref
  2.0 1.4 copy.15.scores_ref
  3.4 0.0 copy-start.1
  3.5 0.0 copy-start
  3.5 157.8 %shard_map.95 = (bf16[128,3584]{1,0:T(8,128)(2,1)}, f32[8,128]{1,0:T(8,128)}) custom-call(s32[128,2]{1,0:T(8,128)} %copy.14.ids_ref, f32[128,2]{1,0:T(8,128)} %copy.15.scores_ref, bf16[128,3584]{1,0:T(8,128)(2,1)} %x_hbm.1, bf16[3584,256]{1,0:T(8,128)(2,1)} %bitcast.6, bf16[3584,256]{1,0:T(8,128)(2,1)} %bitcast.7, bf16[256,3584]{1,0:T(8,128)(2,1)} %bitcast.8, ...), custom_call_target="tpu_custom_call" | custom-call | tf_op jit(solution)/shard_map/pallas_call | solution.py:629
  161.3 0.0 copy-done.1
  161.3 0.7 select_reduce_fusion
  162.0 0.0 copy-done
  162.0 0.6 subtract_multiply_fusion
  162.6 2.2 %copy.17 = bf16[128,3584]{1,0:T(8,128)(2,1)} copy(bf16[128,3584]{1,0:T(8,128)(2,1)} %get-tuple-element.12) | data formatting | bytes 1835008
  (2 shorter events, 0.0 us)
Async XLA Ops:
  3.4 157.8 %copy-start.1 = (s32[128,2]{0,1:T(2,128)S(1)}, s32[128,2]{0,1:T(2,128)}, u32[]{:S(2)}) copy-start(s32[128,2]{0,1:T(2,128)} %param.9) | copy-start | bytes 3076
  3.5 158.5 %copy-start = (f32[128,2]{0,1:T(2,128)S(1)}, f32[128,2]{0,1:T(2,128)}, u32[]{:S(2)}) copy-start(f32[128,2]{0,1:T(2,128)} %param.10) | copy-start | bytes 3076

commit v4 on v2

--- a/solution.py
+++ b/solution.py
@@ -323,9 +323,6 @@
     take_up(2)
     take_down(2)
     ready = 4
-    lax.fori_loop(0, ready, lambda k, _: (pass_gu(k), 0)[1], 0)
-    take_up(3)
-    take_down(3)
     for copy in local:
         copy.wait()
     y_arrival(1).wait_recv()
@@ -334,7 +331,8 @@
     for o in range(1, 8):
         remote(META.at[o], META.at[o], meta_send.at[o], meta_recv.at[o], column(o)).wait_recv()
     sib_arrival(0, z).wait_recv()
-    for d in range(1, ZS):
+
+    def chunk_ready(d):
         @pl.when(z - d >= 0)
         def _():
             sib_arrival(d, z - d).wait_recv()
@@ -342,6 +340,12 @@
         @pl.when(z + d <= ZS - 1)
         def _():
             sib_arrival(3 + d, z + d).wait_recv()
+
+    def job(s):
+        order = ((0, 1, 2, 3), (1, 0, 2, 3), (2, 3, 1, 0), (3, 2, 1, 0))
+        return jnp.where(
+            z == 0, order[0][s], jnp.where(z == 1, order[1][s], jnp.where(z == 2, order[2][s], order[3][s]))
+        )
 
     slot_lane = lax.broadcasted_iota(jnp.int32, (T, CAP), 1).astype(F32)
     row8 = lax.broadcasted_iota(jnp.int32, (8, T), 0)
@@ -375,7 +379,19 @@
             PRS[zz * 2 + cc] = jnp.where(row8 == expert, total, 0.0)
         return 0
 
-    lax.fori_loop(0, ZS, hidden, 0)
+    hidden(job(0), 0)
+    chunk_ready(1)
+    pass_gu(0)
+    hidden(job(1), 0)
+    chunk_ready(2)
+    pass_gu(1)
+    hidden(job(2), 0)
+    pass_gu(2)
+    pass_gu(3)
+    take_up(3)
+    take_down(3)
+    chunk_ready(3)
+    hidden(job(3), 0)
     for o in range(1, 8):
         remote(PRS.at[(me + o) % 8], PRR.at[o], pr_send.at[o], pr_recv.at[o], column(o)).start()
 

time: 156 us -> 156 us (level)
  no operation moved by 1% of the time
where the time goes in v4:
time: 156 us
  Pallas kernels  149 us (96%)
  local copies, waits for them, and re-layouts  4.99 us (3%)
    pallas_call x1, Pallas kernels, fused_on_device(): pl.pallas_call(fused, out_shape=(jax.ShapeDtypeStruct((T, D), BF16), jax....  149 us
    unnamed x7, local copies, waits for them, and re-layouts  4.99 us

profile of v4, /device:TPU:0, one launch (start us, length us, event | category | flops | bytes accessed | tf_op | source)
XLA Modules:
  0.0 155.7 jit_solution(6921703899017145004)
XLA Ops:
  0.6 1.4 copy.14.ids_ref
  2.0 1.4 copy.15.scores_ref
  3.4 0.0 copy-start.1
  3.5 0.0 copy-start
  3.5 148.7 %shard_map.95 = (bf16[128,3584]{1,0:T(8,128)(2,1)}, f32[8,128]{1,0:T(8,128)}) custom-call(s32[128,2]{1,0:T(8,128)} %copy.14.ids_ref, f32[128,2]{1,0:T(8,128)} %copy.15.scores_ref, bf16[128,3584]{1,0:T(8,128)(2,1)} %x_hbm.1, bf16[3584,256]{1,0:T(8,128)(2,1)} %bitcast.6, bf16[3584,256]{1,0:T(8,128)(2,1)} %bitcast.7, bf16[256,3584]{1,0:T(8,128)(2,1)} %bitcast.8, ...), custom_call_target="tpu_custom_call" | custom-call | tf_op jit(solution)/shard_map/pallas_call | solution.py:559
  152.2 0.0 copy-done.1
  152.2 0.7 select_reduce_fusion
  152.9 0.0 copy-done
  152.9 0.6 subtract_multiply_fusion
  153.5 2.2 %copy.17 = bf16[128,3584]{1,0:T(8,128)(2,1)} copy(bf16[128,3584]{1,0:T(8,128)(2,1)} %get-tuple-element.12) | data formatting | bytes 1835008
  (2 shorter events, 0.0 us)
Async XLA Ops:
  3.4 148.7 %copy-start.1 = (s32[128,2]{0,1:T(2,128)S(1)}, s32[128,2]{0,1:T(2,128)}, u32[]{:S(2)}) copy-start(s32[128,2]{0,1:T(2,128)} %param.9) | copy-start | bytes 3076
  3.5 149.4 %copy-start = (f32[128,2]{0,1:T(2,128)S(1)}, f32[128,2]{0,1:T(2,128)}, u32[]{:S(2)}) copy-start(f32[128,2]{0,1:T(2,128)} %param.10) | copy-start | bytes 3076
